TPU v7x, 256 devices: a whole 4x4x8 slice. The times are simulated.
256 devices in a mesh: row: 8 (over z_lo, y), col: 4 (over z_hi), depth: 8 (over x, core).
Axes of the slice: x: 4, y: 4, z: 8 (z_hi: 4, z_lo: 2; z = z_hi * 2 + z_lo), core: 2. Of those that a mesh axis runs over, the one named last changes fastest.
Arguments:
- tokens: bfloat16 [2048, 12288], P(('row', 'col'), 'depth'), may hold values from -6 to 6
- weight: bfloat16 [12288, 24576], P('depth', ('row', 'col')), may hold values from -5 to 5
- moment: bfloat16 [12288, 24576], P('depth', ('row', 'col')), may hold values from -0.59765625 to 0.59765625
- upstream: bfloat16 [8, 256, 24576], P(None, 'col', ('row', 'depth')), may hold values from -24 to 24
Outputs:
- activated: bfloat16 [8, 256, 24576], P(None, 'col', ('row', 'depth'))
- new_weight: bfloat16 [12288, 24576], P('depth', ('row', 'col'))
- new_moment: bfloat16 [12288, 24576], P('depth', ('row', 'col'))
All inputs are finite; a program needn't handle non-finite values.
Results may differ from a plain program's by a relative error of at most 0.015.
Values may be sent and summed in bfloat16 or wider, within the bound.
A program may use at most 64 MiB of HBM per device.

v0:
```python
import jax
import jax.numpy as jnp
from jax import lax
from jax.sharding import PartitionSpec as P

D = 12288
gelu_coef = 0.7978845608028654
cubic_coef = 0.044715
lion_rate = 0.5
decay_rate = 0.1
beta_one = 0.9
beta_two = 0.99
smooth_tau = 0.1


def gelu_pair(preact):
    tangent = jnp.tanh(gelu_coef * (preact + cubic_coef * preact * preact * preact))
    gelu_value = 0.5 * preact * (1.0 + tangent)
    gelu_slope = 0.5 * (1.0 + tangent) + 0.5 * preact * (1.0 - tangent * tangent) * gelu_coef * (
        1.0 + 3.0 * cubic_coef * preact * preact
    )
    return (gelu_value, gelu_slope)


def shards(tokens, weight, moment, upstream):
    row_count = lax.axis_size("row")
    tok_rows = tokens.shape[0]
    fan_scale = D ** (-0.5)
    gathered = lax.all_gather(tokens, "row", axis=0, tiled=True)
    partial_value = jnp.dot(
        gathered,
        lax.all_gather(weight, "col", axis=1, tiled=True),
        preferred_element_type=jnp.float32,
    )
    summed = lax.psum_scatter(
        partial_value.astype(jnp.bfloat16), "depth", scatter_dimension=1, tiled=True
    ).astype(jnp.float32)
    gelu_value, gelu_slope = gelu_pair(summed * fan_scale)
    activated = gelu_value.astype(jnp.bfloat16)
    upstream_flat = upstream.reshape(row_count * tok_rows, upstream.shape[2]).astype(jnp.float32)
    local_grad = (upstream_flat * gelu_slope).astype(jnp.bfloat16)
    act_grad = lax.all_gather(local_grad, "depth", axis=1, tiled=True)
    grad_panel = lax.dot_general(
        gathered, act_grad, (((0,), (0,)), ((), ())), preferred_element_type=jnp.float32
    )
    grad_sum = lax.psum_scatter(
        grad_panel.astype(jnp.bfloat16), "col", scatter_dimension=1, tiled=True
    ).astype(jnp.float32)
    grad_full = grad_sum * fan_scale
    moment_f = moment.astype(jnp.float32)
    weight_f = weight.astype(jnp.float32)
    blended = beta_one * moment_f + (1.0 - beta_one) * grad_full
    update = blended / jnp.sqrt(blended * blended + smooth_tau * smooth_tau)
    new_weight = (weight_f - lion_rate * (update + decay_rate * weight_f)).astype(jnp.bfloat16)
    new_moment = (beta_two * moment_f + (1.0 - beta_two) * grad_full).astype(jnp.bfloat16)
    activated = activated.reshape(upstream.shape[0], upstream.shape[1], activated.shape[1])
    return (activated, new_weight, new_moment)


def solution(mesh):
    placed = (
        P(("row", "col"), "depth"),
        P("depth", ("row", "col")),
        P("depth", ("row", "col")),
        P(None, "col", ("row", "depth")),
    )
    return jax.shard_map(
        shards,
        mesh=mesh,
        in_specs=placed,
        out_specs=(
            P(None, "col", ("row", "depth")),
            P("depth", ("row", "col")),
            P("depth", ("row", "col")),
        ),
        check_vma=False,
    )
```

profile of v0, /device:TPU:2, one launch (start us, length us, event | category | flops | bytes accessed | tf_op | source)
XLA Modules:
  0.0 509.9 jit_solution(10022676626198729526)
XLA Ops:
  7.2 0.0 all-gather.4.cloned.1.call-start
  7.2 0.7 all-gather.4.cloned.1.call-update
  7.9 0.0 all-gather.6.cloned.1.call-start
  7.9 0.7 all-gather.6.cloned.1.call-update
  8.6 0.0 reduce-scatter.7.cloned.1.call-start
  8.7 47.2 %all-gather.4.cloned.1.call-done = bf16[512,1536]{1,0:T(8,128)(2,1)} async-done(((bf16[64,1536]{1,0:T(8,128)(2,1)}), bf16[512,1536]{1,0:T(8,128)(2,1)}) %all-gather.4.cloned.1.call-update) | async-done | bytes 1572880 | tf_op jit(solution)/shard_map/all_gather | solution.py:29
  55.9 173.9 %all-gather.6.cloned.1.call-done = bf16[1536,3072]{1,0:T(8,128)(2,1)} async-done(((bf16[1536,768]{1,0:T(8,128)(2,1)}), bf16[1536,3072]{1,0:T(8,128)(2,1)}) %all-gather.6.cloned.1.call-update) | async-done | bytes 9437200 | tf_op jit(solution)/shard_map/all_gather | solution.py:32
  229.8 8.1 %convolution_convert_fusion.1 = bf16[512,3072]{1,0:T(8,128)(2,1)S(1)} fusion(bf16[512,1536]{1,0:T(8,128)(2,1)} %all-gather.4.cloned.1.call-done, bf16[1536,3072]{1,0:T(8,128)(2,1)} %all-gather.6.cloned.1.call-done), kind=kOutput, calls=%fused_computation.14 | convolution fusion | flops 4833411072 | bytes 14155776 | tf_op jit(solution)/shard_map/dot_general | solution.py:30
  237.9 0.0 copy-start.3
  237.9 2.8 copy.15
  240.7 0.0 copy-start.4
  240.7 0.0 reduce-scatter.7.cloned.1.call-update
  240.8 0.0 all-gather.8.cloned.1.call-start
  240.8 33.4 %reduce-scatter.7.cloned.1.call-done = bf16[384,512]{1,0:T(8,128)(2,1)} async-done(((bf16[3072,512]{1,0:T(8,128)(2,1)}), bf16[384,512]{1,0:T(8,128)(2,1)}) %reduce-scatter.7.cloned.1.call-update) | async-done | bytes 393232
  274.2 1.2 copy.16
  275.4 0.0 copy-done.3
  275.4 1.5 fusion.18
  277.0 0.0 all-gather.8.cloned.1.call-update
  277.0 0.0 reduce-scatter.5.cloned.1.call-start
  277.0 31.8 %all-gather.8.cloned.1.call-done = bf16[512,3072]{1,0:T(8,128)(2,1)} async-done(((bf16[512,384]{1,0:T(8,128)(2,1)}), bf16[512,3072]{1,0:T(8,128)(2,1)}) %all-gather.8.cloned.1.call-update) | async-done | bytes 3145744 | tf_op jit(solution)/shard_map/all_gather | solution.py:42
  308.8 0.0 copy-done.4
  308.8 9.6 %fusion = bf16[1536,3072]{0,1:T(8,128)(2,1)} fusion(bf16[512,3072]{1,0:T(8,128)(2,1)} %all-gather.8.cloned.1.call-done, bf16[512,1536]{1,0:T(8,128)(2,1)S(1)} %copy-done.4), kind=kOutput, calls=%fused_computation.1 | convolution fusion | flops 4836556800 | bytes 14155776 | tf_op jit(solution)/shard_map/dot_general | solution.py:43
  318.4 0.0 copy-start
  318.4 0.0 reduce-scatter.5.cloned.1.call-update
  318.4 1.6 copy-done
  320.1 2.4 copy.11
  322.5 0.0 copy-start.1
  322.5 4.4 copy.12
  326.9 163.8 %reduce-scatter.5.cloned.1.call-done = bf16[1536,768]{0,1:T(8,128)(2,1)} async-done(((bf16[1536,3072]{0,1:T(8,128)(2,1)}), bf16[1536,768]{0,1:T(8,128)(2,1)}) %reduce-scatter.5.cloned.1.call-update) | async-done | bytes 2359312 | tf_op jit(solution)/shard_map/reduce_scatter | solution.py:46
  490.7 0.0 copy-done.1
  490.7 5.9 %fusion.6 = (bf16[1536,768]{0,1:T(8,128)(2,1)}, bf16[1536,768]{0,1:T(8,128)(2,1)}) fusion(bf16[1536,768]{0,1:T(8,128)(2,1)} %copy.12, bf16[1536,768]{0,1:T(8,128)(2,1)} %reduce-scatter.5.cloned.1.call-done, bf16[1536,768]{0,1:T(8,128)(2,1)S(1)} %copy-done.1), kind=kLoop, calls=%fused_computation.13 | loop fusion | flops 21233664 | bytes 11796480 | tf_op jit(solution)/shard_map/convert_element_type | solution.py:55
  496.6 0.0 copy-start.2
  496.6 4.4 copy.13
  501.0 0.0 copy-done.2
  501.0 2.4 copy.14
Async XLA Ops:
  7.2 48.8 %all-gather.4.cloned.1.call-start = ((), (), s32[]{:S(2)}) async-start(), calls=%async_computation.2 | async-start | bytes 1769472 | tf_op jit(solution)/shard_map/all_gather | solution.py:29
  7.9 221.9 %all-gather.6.cloned.1.call-start = ((), (), s32[]{:S(2)}) async-start(), calls=%async_computation.3 | async-start | bytes 11796480 | tf_op jit(solution)/shard_map/all_gather | solution.py:32
  8.6 265.6 %reduce-scatter.7.cloned.1.call-start = ((), (), s32[]{:S(2)}) async-start(), calls=%async_computation.6 | async-start | bytes 3538944
  237.9 37.5 %copy-start.3 = (bf16[8,64,384]{2,1,0:T(8,128)(2,1)S(1)}, bf16[8,64,384]{2,1,0:T(8,128)(2,1)}, u32[]{:S(2)}) copy-start(bf16[8,64,384]{2,1,0:T(8,128)(2,1)} %param.7) | copy-start | bytes 1179652
  240.7 68.1 %copy-start.4 = (bf16[512,1536]{1,0:T(8,128)(2,1)S(1)}, bf16[512,1536]{1,0:T(8,128)(2,1)}, u32[]{:S(2)}) copy-start(bf16[512,1536]{1,0:T(8,128)(2,1)} %all-gather.4.cloned.1.call-done) | copy-start | bytes 4718596
  240.8 68.0 %all-gather.8.cloned.1.call-start = ((), (), s32[]{:S(2)}) async-start(), calls=%async_computation.4 | async-start | bytes 3538944 | tf_op jit(solution)/shard_map/all_gather | solution.py:42
  277.0 213.7 %reduce-scatter.5.cloned.1.call-start = ((), (), s32[]{:S(2)}) async-start(), calls=%async_computation.5 | async-start | bytes 11796480 | tf_op jit(solution)/shard_map/reduce_scatter | solution.py:46
  318.4 1.7 copy-start
  322.5 168.2 %copy-start.1 = (bf16[1536,768]{0,1:T(8,128)(2,1)S(1)}, bf16[1536,768]{0,1:T(8,128)(2,1)}, u32[]{:S(2)}) copy-start(bf16[1536,768]{0,1:T(8,128)(2,1)} %copy.11) | copy-start | bytes 7077892
  496.6 4.4 copy-start.2
Sparse Core Ops, SparseCore 0:
  9.8 46.0 all-gather.3
  57.7 172.0 all-gather.5
  240.9 33.2 reduce-scatter.6
  277.1 31.6 all-gather.7
  318.5 172.1 reduce-scatter.4
where the time goes:
time: 510 us
  waiting for transfers between devices  452 us (89%)
  local copies, waits for them, and re-layouts  19.4 us (4%)
  matrix products  17.7 us (3%)
  between operations  13.8 us (3%)
  other arithmetic  7.4 us (1%)
    all_gather x1, waiting for transfers between devices, shards(): lax.all_gather(weight, 'col', axis=1, tiled=True)  174 us
    reduce_scatter x1, waiting for transfers between devices, shards(): lax.psum_scatter(grad_panel.astype(jnp.bfloat16), 'col', scatter_dimensio...  164 us
    all_gather x1, waiting for transfers between devices, shards(): gathered = lax.all_gather(tokens, 'row', axis=0, tiled=True)  47.2 us
    unnamed x6, waiting for transfers between devices  34.8 us
    all_gather x1, waiting for transfers between devices, shards(): act_grad = lax.all_gather(local_grad, 'depth', axis=1, tiled=True)  31.8 us
    unnamed x16, local copies, waits for them, and re-layouts  19.4 us
  transfers between devices with their start and end apart: 5, of which 5 were waited for; matrix products, arithmetic and copies ran while one was open for 1% of the time, Pallas kernels for 0%

commit v1 on v0

--- a/solution.py
+++ b/solution.py
@@ -29,7 +29,9 @@
     gathered = lax.all_gather(tokens, "row", axis=0, tiled=True)
     partial_value = jnp.dot(
         gathered,
-        lax.all_gather(weight, "col", axis=1, tiled=True),
+        jnp.concatenate(
+            lax.all_to_all(jnp.stack([weight] * lax.axis_size("col")), "col", 0, 0), axis=1
+        ),
         preferred_element_type=jnp.float32,
     )
     summed = lax.psum_scatter(

time: 510 us -> 527 us (1.033)
  starting transfers between devices: 0.2 us -> 8.58 us
    all_gather x1 -> x0, waiting for transfers between devices: 174 us -> none  [shards(): lax.all_gather(weight, 'col', axis=1, tiled=True)]
    all_to_all x0 -> x1, waiting for transfers between devices: none -> 125 us  [shards(): lax.all_to_all(jnp.stack([weight] * lax.axis_size('col')), 'col', 0, 0)]
    all_gather x1, waiting for transfers between devices: 47.2 us -> 96.9 us  [shards(): gathered = lax.all_gather(tokens, 'row', axis=0, tiled=True)]
    all_to_all x0 -> x1, starting transfers between devices: none -> 8.46 us  [shards(): lax.all_to_all(jnp.stack([weight] * lax.axis_size('col')), 'col', 0, 0)]
    unnamed x6 -> x5, waiting for transfers between devices: 34.8 us -> 32.4 us
    unnamed x16 -> x10, local copies, waits for them, and re-layouts: 19.4 us -> 19.9 us
where the time goes in v1:
time: 527 us; the launch traced here: 525 us
  waiting for transfers between devices  453 us (86%)
  local copies, waits for them, and re-layouts  24.3 us (5%)
  matrix products  18.7 us (4%)
  between operations  13.8 us (3%)
  starting transfers between devices  8.58 us (2%)
  other arithmetic  7.39 us (1%)
    reduce_scatter x1, waiting for transfers between devices, shards(): lax.psum_scatter(grad_panel.astype(jnp.bfloat16), 'col', scatter_dimensio...  166 us
    all_to_all x1, waiting for transfers between devices, shards(): lax.all_to_all(jnp.stack([weight] * lax.axis_size('col')), 'col', 0, 0)  125 us
    all_gather x1, waiting for transfers between devices, shards(): gathered = lax.all_gather(tokens, 'row', axis=0, tiled=True)  96.9 us
    unnamed x5, waiting for transfers between devices  32.4 us
    all_gather x1, waiting for transfers between devices, shards(): act_grad = lax.all_gather(local_grad, 'depth', axis=1, tiled=True)  31.7 us
    unnamed x10, local copies, waits for them, and re-layouts  19.9 us
  transfers between devices with their start and end apart: 5, of which 5 were waited for; matrix products, arithmetic and copies ran while one was open for 1% of the time, Pallas kernels for 0%

profile of v1, /device:TPU:2, one launch (start us, length us, event | category | flops | bytes accessed | tf_op | source)
XLA Modules:
  0.0 525.2 jit_solution(7104985426650204329)
XLA Ops:
  7.2 2.8 copy.16
  10.0 4.4 stack.2
  14.4 8.5 %all-to-all-start = ((bf16[4,1536,768]{1,2,0:T(8,128)(2,1)}), bf16[4,1536,768]{1,2,0:T(8,128)(2,1)}, u32[]{:S(2)}, u32[]{:S(2)}) async-start(bf16[4,1536,768]{1,2,0:T(8,128)(2,1)} %stack.2), calls=%async_computation | async-start | bytes 18874368 | tf_op jit(solution)/shard_map/all_to_all | solution.py:33
  22.8 0.0 all-gather.3.cloned.1.call-start
  22.9 0.7 all-gather.3.cloned.1.call-update
  23.6 0.0 reduce-scatter.7.cloned.1.call-start
  23.6 96.9 %all-gather.3.cloned.1.call-done = bf16[512,1536]{1,0:T(8,128)(2,1)} async-done(((bf16[64,1536]{1,0:T(8,128)(2,1)}), bf16[512,1536]{1,0:T(8,128)(2,1)}) %all-gather.3.cloned.1.call-update) | async-done | bytes 1572880 | tf_op jit(solution)/shard_map/all_gather | solution.py:29
  120.5 125.3 %all-to-all-done = bf16[4,1536,768]{1,2,0:T(8,128)(2,1)} async-done(((bf16[4,1536,768]{1,2,0:T(8,128)(2,1)}), bf16[4,1536,768]{1,2,0:T(8,128)(2,1)}, u32[]{:S(2)}, u32[]{:S(2)}) %all-to-all-start) | async-done | bytes 9437216 | tf_op jit(solution)/shard_map/all_to_all | solution.py:33
  245.8 9.3 %convolution_convert_fusion.1 = bf16[512,3072]{1,0:T(8,128)(2,1)} fusion(bf16[512,1536]{1,0:T(8,128)(2,1)} %all-gather.3.cloned.1.call-done, bf16[1536,3072]{0,1:T(8,128)(2,1)} %bitcast.1), kind=kOutput, calls=%fused_computation.14 | convolution fusion | flops 4833411072 | bytes 14155776 | tf_op jit(solution)/shard_map/dot_general | solution.py:30
  255.1 0.0 copy-start.1
  255.1 4.7 copy.21
  259.8 0.0 reduce-scatter.7.cloned.1.call-update
  259.8 0.0 all-gather.5.cloned.1.call-start
  259.9 31.7 %reduce-scatter.7.cloned.1.call-done = bf16[384,512]{1,0:T(8,128)(2,1)} async-done(((bf16[3072,512]{1,0:T(8,128)(2,1)}), bf16[384,512]{1,0:T(8,128)(2,1)}) %reduce-scatter.7.cloned.1.call-update) | async-done | bytes 393232
  291.5 1.2 copy.22
  292.7 0.0 copy-done.1
  292.7 1.5 fusion.18
  294.3 0.0 all-gather.5.cloned.1.call-update
  294.3 0.0 reduce-scatter.5.cloned.1.call-start
  294.4 31.7 %all-gather.5.cloned.1.call-done = bf16[512,3072]{1,0:T(8,128)(2,1)} async-done(((bf16[512,384]{1,0:T(8,128)(2,1)}), bf16[512,3072]{1,0:T(8,128)(2,1)}) %all-gather.5.cloned.1.call-update) | async-done | bytes 3145744 | tf_op jit(solution)/shard_map/all_gather | solution.py:44
  326.1 9.4 %fusion = bf16[1536,3072]{0,1:T(8,128)(2,1)} fusion(bf16[512,3072]{1,0:T(8,128)(2,1)} %all-gather.5.cloned.1.call-done, bf16[512,1536]{1,0:T(8,128)(2,1)} %all-gather.3.cloned.1.call-done), kind=kOutput, calls=%fused_computation.1 | convolution fusion | flops 4836556800 | bytes 14155776 | tf_op jit(solution)/shard_map/dot_general | solution.py:45
  335.5 0.0 reduce-scatter.5.cloned.1.call-update
  335.5 4.3 copy.18
  339.8 166.2 %reduce-scatter.5.cloned.1.call-done = bf16[1536,768]{0,1:T(8,128)(2,1)} async-done(((bf16[1536,3072]{0,1:T(8,128)(2,1)}), bf16[1536,768]{0,1:T(8,128)(2,1)}) %reduce-scatter.5.cloned.1.call-update) | async-done | bytes 2359312 | tf_op jit(solution)/shard_map/reduce_scatter | solution.py:48
  506.0 5.9 %fusion.6 = (bf16[1536,768]{0,1:T(8,128)(2,1)}, bf16[1536,768]{0,1:T(8,128)(2,1)}) fusion(bf16[1536,768]{0,1:T(8,128)(2,1)} %copy.18, bf16[1536,768]{0,1:T(8,128)(2,1)} %reduce-scatter.5.cloned.1.call-done, bf16[1536,768]{0,1:T(8,128)(2,1)S(1)} %copy.16), kind=kLoop, calls=%fused_computation.13 | loop fusion | flops 21233664 | bytes 11796480 | tf_op jit(solution)/shard_map/convert_element_type | solution.py:57
  511.9 0.0 copy-start
  511.9 4.4 copy.19
  516.3 0.0 copy-done
  516.3 2.4 copy.20
Async XLA Ops:
  14.4 231.4 %all-to-all-start = ((bf16[4,1536,768]{1,2,0:T(8,128)(2,1)}), bf16[4,1536,768]{1,2,0:T(8,128)(2,1)}, u32[]{:S(2)}, u32[]{:S(2)}) async-start(bf16[4,1536,768]{1,2,0:T(8,128)(2,1)} %stack.2), calls=%async_computation | async-start | bytes 18874368 | tf_op jit(solution)/shard_map/all_to_all | solution.py:33
  22.8 97.7 %all-gather.3.cloned.1.call-start = ((), (), s32[]{:S(2)}) async-start(), calls=%async_computation.3 | async-start | bytes 1769472 | tf_op jit(solution)/shard_map/all_gather | solution.py:29
  23.6 268.0 %reduce-scatter.7.cloned.1.call-start = ((), (), s32[]{:S(2)}) async-start(), calls=%async_computation.6 | async-start | bytes 3538944
  255.1 37.6 %copy-start.1 = (bf16[8,64,384]{2,1,0:T(8,128)(2,1)S(1)}, bf16[8,64,384]{2,1,0:T(8,128)(2,1)}, u32[]{:S(2)}) copy-start(bf16[8,64,384]{2,1,0:T(8,128)(2,1)} %param.7) | copy-start | bytes 1179652
  259.8 66.3 %all-gather.5.cloned.1.call-start = ((), (), s32[]{:S(2)}) async-start(), calls=%async_computation.4 | async-start | bytes 3538944 | tf_op jit(solution)/shard_map/all_gather | solution.py:44
  294.3 211.7 %reduce-scatter.5.cloned.1.call-start = ((), (), s32[]{:S(2)}) async-start(), calls=%async_computation.5 | async-start | bytes 11796480 | tf_op jit(solution)/shard_map/reduce_scatter | solution.py:48
  511.9 4.4 copy-start
Sparse Core Ops, SparseCore 0:
  25.5 95.0 all-gather.2
  259.9 31.5 reduce-scatter.6
  294.4 31.6 all-gather.4
  335.6 170.3 reduce-scatter.4
